TPU v7x, 32 devices: a whole 2x2x4 slice. The times are simulated.
32 devices in a mesh: kx: 4 (over y, x), ky: 8 (over z, core).
Axes of the slice: x: 2, y: 2, z: 4, core: 2. Of those that a mesh axis runs over, the one named last changes fastest.
Arguments:
- states: bfloat16 [32, 4096, 128], P(('kx', 'ky')), may hold values from -6 to 6
- energies: bfloat16 [32, 128], P(('kx', 'ky')), may hold values from -2 to 2
- external: float32 [1, 4096], replicated, may hold values from -6 to 6
- reorder: int32 [2, 32, 4096], P(None, ('kx', 'ky')), may hold values from 0 to 4095, each once within a row
Outputs:
- band_response: float32 [32, 2, 1, 128, 128], P(('kx', 'ky'))
- density: float32 [2, 1, 4096], replicated
Inputs may be any that keep to these rules, and one draw needn't show every extreme that they name: Each row reorder[q, k] is a permutation of the 4096 grid components.
All inputs are finite; a program needn't handle non-finite values.
Results may differ from a plain program's by a relative error of at most 0.0029.
Values may be sent and summed in bfloat16 or wider, within the bound.
A program may use at most 64 MiB of HBM per device.

v0:
```python
import math

import jax
import jax.numpy as jnp
from jax import lax
from jax.sharding import PartitionSpec as P

GX = 64
GY = 64
NQ = 2
ITERS = 2


SMEAR = 0.5
FERMI = 0.0
SCREEN = 4.0


def passed_along(value, axis, steps):
    count = lax.axis_size(axis)
    pairs = [(source, (source + steps) % count) for source in range(count)]
    return lax.ppermute(value, axis, pairs)


def hartley_table(length):
    positions = jnp.arange(length, dtype=jnp.int32)
    phases = positions[:, None] * positions[None, :] % length
    angles = phases.astype(jnp.float32) * (2.0 * math.pi / length)
    return (jnp.cos(angles) + jnp.sin(angles)) / math.sqrt(length)


def screening(len_x, len_y):
    freq_x = jnp.arange(len_x, dtype=jnp.int32)
    freq_x = jnp.minimum(freq_x, len_x - freq_x).astype(jnp.float32)
    freq_y = jnp.arange(len_y, dtype=jnp.int32)
    freq_y = jnp.minimum(freq_y, len_y - freq_y).astype(jnp.float32)
    return 1.0 / (1.0 + (freq_x[:, None] ** 2 + freq_y[None, :] ** 2) / SCREEN)


def coulomb(density):
    fields = density.reshape(density.shape[:-1] + (GX, GY))
    table_x = hartley_table(GX)
    table_y = hartley_table(GY)
    spectra = jnp.einsum(
        "pi,abij,jq->abpq", table_x, fields, table_y, precision=lax.Precision.HIGHEST
    )
    spectra = spectra * screening(GX, GY)
    result = jnp.einsum(
        "pi,abij,jq->abpq", table_x, spectra, table_y, precision=lax.Precision.HIGHEST
    )
    return result.reshape(density.shape)


def occupation(energy):
    return 1.0 / (1.0 + jnp.exp((energy - FERMI) / SMEAR))


def respond(orbital, energy, far_states, far_energy, potential):
    energy = energy.astype(jnp.float32)
    far_energy = far_energy.astype(jnp.float32)
    weighted = (potential[:, :, None] * orbital[None].astype(jnp.float32)).astype(jnp.bfloat16)
    band_mats = jnp.einsum("gm,agn->amn", far_states, weighted, preferred_element_type=jnp.float32)
    band_mats = band_mats * (1.0 / math.sqrt(orbital.shape[0]))
    gap_matrix = far_energy[:, None] - energy[None, :]
    weight = (
        (occupation(energy)[None, :] - occupation(far_energy)[:, None])
        * gap_matrix
        / (gap_matrix * gap_matrix + SMEAR * SMEAR)
    )
    response = weight[None] * band_mats
    response_low = response.astype(jnp.bfloat16)
    orbitals_out = jnp.einsum(
        "gm,amn->agn", far_states, response_low, preferred_element_type=jnp.float32
    )
    orbitals_out = orbitals_out * (1.0 / math.sqrt(orbital.shape[1]))
    contrib = jnp.sum(orbital[None].astype(jnp.float32) * orbitals_out, axis=2)
    return (response, contrib)


def partner_of(q_index, orbital, energy, reorder):
    if q_index == 0:
        far_states, far_energy = passed_along((orbital, energy), "kx", -1)
    else:
        far_states, far_energy = passed_along((orbital, energy), "ky", -1)
    return (jnp.take(far_states, reorder[q_index, 0], axis=0), far_energy)


def shards(states, energies, external, reorder):
    orbital = states[0]
    energy = energies[0]
    kpoint_count = lax.axis_size("kx") * lax.axis_size("ky")
    grid_size = orbital.shape[0]
    potential = jnp.broadcast_to(external[None], (NQ, external.shape[0], grid_size))
    fetched_all = [None for q_index in range(NQ)]
    fetched_all = [partner_of(q_index, orbital, energy, reorder) for q_index in range(NQ)]
    for rounds in range(ITERS):
        responses = []
        density_parts = []
        for q_index in range(NQ):
            far_states, far_energy = fetched_all[q_index]
            response, contrib = respond(orbital, energy, far_states, far_energy, potential[q_index])
            responses.append(response)
            density_parts.append(contrib)
        density = jnp.stack(density_parts)
        density = lax.psum(density, ("kx", "ky"))
        density = density * (1.0 / math.sqrt(kpoint_count))
        if rounds + 1 < ITERS:
            potential = external[None] + coulomb(density)
    return (jnp.stack(responses)[None], density)


def solution(mesh):
    return jax.shard_map(
        shards,
        mesh=mesh,
        in_specs=(
            P(("kx", "ky"), None, None),
            P(("kx", "ky"), None),
            P(),
            P(None, ("kx", "ky"), None),
        ),
        out_specs=(P(("kx", "ky"), None, None, None, None), P()),
        check_vma=False,
    )
```

profile of v0, /device:TPU:0, one launch (start us, length us, event | category | flops | bytes accessed | tf_op | source)
XLA Modules:
  0.0 146.7 jit_solution(7657217151803382496)
XLA Ops:
  0.6 3.9 %collective-permute-start.1 = (bf16[4096,128]{1,0:T(8,128)(2,1)}, bf16[4096,128]{1,0:T(8,128)(2,1)S(1)}, u32[]{:S(2)}, u32[]{:S(2)}) collective-permute-start(bf16[4096,128]{1,0:T(8,128)(2,1)} %bitcast.128), channel_id=1, source_target_pairs={{0,24},{8,0},{16,8},{24,16},{1,25},{9,1},{17,9},{25,17},{2,26},{10... | collective-permute-start | bytes 3145736 | tf_op jit(solution)/shard_map/ppermute | solution.py:22
  4.6 2.8 %collective-permute-start.3 = (bf16[4096,128]{1,0:T(8,128)(2,1)}, bf16[4096,128]{1,0:T(8,128)(2,1)S(1)}, u32[]{:S(2)}, u32[]{:S(2)}) collective-permute-start(bf16[4096,128]{1,0:T(8,128)(2,1)} %bitcast.129), channel_id=1, source_target_pairs={{0,7},{1,0},{2,1},{3,2},{4,3},{5,4},{6,5},{7,6},{8,15},{9,8},{10,9... | collective-permute-start | bytes 3145736 | tf_op jit(solution)/shard_map/ppermute | solution.py:22
  7.3 0.5 collective-permute-start
  7.9 0.7 collective-permute-start.2
  8.5 0.7 fusion.100
  9.3 0.1 add_divide_fusion
  9.4 0.7 convert_bitcast_fusion
  10.1 0.7 divide_bitcast_fusion
  10.8 2.3 %copy.6 = bf16[1,4096,128]{1,2,0:T(8,128)(2,1)} copy(bf16[1,4096,128]{2,1,0:T(8,128)(2,1)} %param.6) | data formatting | bytes 2097152 | tf_op args[0]
  13.0 14.3 %collective-permute-done = bf16[128]{0:T(256)(128)(2,1)S(1)} collective-permute-done((bf16[128]{0:T(256)(128)(2,1)}, bf16[128]{0:T(256)(128)(2,1)S(1)}, u32[]{:S(2)}, u32[]{:S(2)}) %collective-permute-start) | collective-permute-done | bytes 288 | tf_op jit(solution)/shard_map/ppermute | solution.py:22
  27.3 0.0 collective-permute-done.2
  27.3 0.0 copy-start.1
  27.4 0.0 collective-permute-done.1
  27.4 12.1 %gather_fusion = bf16[4096,128]{1,0:T(8,128)(2,1)S(1)} fusion(bf16[4096,128]{1,0:T(8,128)(2,1)S(1)} %collective-permute-done.1, s32[4096]{0:T(1024)S(1)} %fusion.71), kind=kCustom, calls=%fused_computation.clone | custom fusion | bytes 2113536 | tf_op jit(solution)/shard_map/jit(_take)/gather | solution.py:85
  39.5 0.0 copy-done.1
  39.5 3.1 %fusion.7 = f32[4096]{0:T(1024)S(1)} fusion(bf16[1,4096,128]{1,2,0:T(8,128)(2,1)} %copy.6, f32[4096]{0:T(1024)S(1)} %bitcast.136, f32[128]{0:T(128)S(1)} %convert_bitcast_fusion, f32[128]{0:T(128)S(1)} %convert_element_type.71, f32[128]{0:T(128)S(1)} %add_divide_fusion.2, f32[128]{0:T(128)S(1)} %divide_bitcast_fusion, ...), kind=kOutput, calls=%fused_computation.20 | convolution fusion | flops 273297408 | bytes 2136064 | tf_op jit(solution)/shard_map/gm,amn->agn/dot_general | solution.py:72
  42.6 0.0 collective-permute-done.3
  42.6 12.1 %gather_fusion.1 = bf16[4096,128]{1,0:T(8,128)(2,1)S(1)} fusion(bf16[4096,128]{1,0:T(8,128)(2,1)S(1)} %collective-permute-done.3, s32[4096]{0:T(1024)S(1)} %fusion.72), kind=kCustom, calls=%fused_computation.1.clone | custom fusion | bytes 2113536 | tf_op jit(solution)/shard_map/jit(_take)/gather | solution.py:85
  54.8 3.1 %fusion.8 = f32[4096]{0:T(1024)S(1)} fusion(bf16[1,4096,128]{1,2,0:T(8,128)(2,1)} %copy.6, f32[4096]{0:T(1024)S(1)} %bitcast.137, f32[128]{0:T(128)S(1)} %convert_element_type.75, f32[128]{0:T(128)S(1)} %add_divide_fusion.1, f32[128]{0:T(128)S(1)} %convert_bitcast_fusion, f32[128]{0:T(128)S(1)} %divide_bitcast_fusion, ...), kind=kOutput, calls=%fused_computation.21 | convolution fusion | flops 273297408 | bytes 2136064 | tf_op jit(solution)/shard_map/gm,amn->agn/dot_general | solution.py:72
  57.8 0.0 copy-start
  57.9 41.6 %psum.14 = f32[2,1,4096]{2,1,0:T(1,128)S(1)} all-reduce(f32[2,1,4096]{2,1,0:T(1,128)S(1)} %pad_maximum_fusion), channel_id=1, replica_groups=mesh['kx'=4,'ky'=8] {'kx','ky'}, use_global_device_ids=true, to_apply=%region_2.4 | all-reduce | flops 8192 | bytes 65536 | tf_op jit(solution)/shard_map/psum | solution.py:105
  99.5 0.1 multiply_reduce_fusion
  99.6 0.1 reshape.393
  99.7 0.4 fusion.52
  100.1 0.3 convolution_multiply_fusion.6
  100.4 0.3 fusion.49
  100.8 0.3 fusion.47
  101.1 0.1 reshape.394
  101.3 0.0 copy-done
  101.3 0.8 fusion.14
  102.1 1.1 fusion.9
  103.2 0.8 fusion.12
  104.0 1.1 fusion.10
  105.1 40.2 %psum.15 = f32[2,1,4096]{2,1,0:T(1,128)S(1)} all-reduce(f32[2,1,4096]{2,1,0:T(1,128)S(1)} %pad_maximum_fusion.1), channel_id=1, replica_groups=mesh['kx'=4,'ky'=8] {'kx','ky'}, use_global_device_ids=true, to_apply=%region_5.7 | all-reduce | flops 8192 | bytes 65536 | tf_op jit(solution)/shard_map/psum | solution.py:105
  145.3 0.7 broadcast_multiply_fusion
  145.9 0.8 copy.7
  (14 shorter events, 0.2 us)
Async XLA Ops:
  0.6 26.7 %collective-permute-start.1 = (bf16[4096,128]{1,0:T(8,128)(2,1)}, bf16[4096,128]{1,0:T(8,128)(2,1)S(1)}, u32[]{:S(2)}, u32[]{:S(2)}) collective-permute-start(bf16[4096,128]{1,0:T(8,128)(2,1)} %bitcast.128), channel_id=1, source_target_pairs={{0,24},{8,0},{16,8},{24,16},{1,25},{9,1},{17,9},{25,17},{2,26},{10... | collective-permute-start | bytes 3145736 | tf_op jit(solution)/shard_map/ppermute | solution.py:22
  4.6 38.0 %collective-permute-start.3 = (bf16[4096,128]{1,0:T(8,128)(2,1)}, bf16[4096,128]{1,0:T(8,128)(2,1)S(1)}, u32[]{:S(2)}, u32[]{:S(2)}) collective-permute-start(bf16[4096,128]{1,0:T(8,128)(2,1)} %bitcast.129), channel_id=1, source_target_pairs={{0,7},{1,0},{2,1},{3,2},{4,3},{5,4},{6,5},{7,6},{8,15},{9,8},{10,9... | collective-permute-start | bytes 3145736 | tf_op jit(solution)/shard_map/ppermute | solution.py:22
  7.3 20.0 %collective-permute-start = (bf16[128]{0:T(256)(128)(2,1)}, bf16[128]{0:T(256)(128)(2,1)S(1)}, u32[]{:S(2)}, u32[]{:S(2)}) collective-permute-start(bf16[128]{0:T(256)(128)(2,1)} %bitcast.145), channel_id=1, source_target_pairs={{0,24},{8,0},{16,8},{24,16},{1,25},{9,1},{17,9},{25,17},{2,26},{10... | collective-permute-start | bytes 776 | tf_op jit(solution)/shard_map/ppermute | solution.py:22
  7.9 19.4 %collective-permute-start.2 = (bf16[128]{0:T(256)(128)(2,1)}, bf16[128]{0:T(256)(128)(2,1)S(1)}, u32[]{:S(2)}, u32[]{:S(2)}) collective-permute-start(bf16[128]{0:T(256)(128)(2,1)} %bitcast.146), channel_id=1, source_target_pairs={{0,7},{1,0},{2,1},{3,2},{4,3},{5,4},{6,5},{7,6},{8,15},{9,8},{10,9... | collective-permute-start | bytes 776 | tf_op jit(solution)/shard_map/ppermute | solution.py:22
  27.3 12.2 %copy-start.1 = (f32[1,4096]{1,0:T(1,128)S(1)}, f32[1,4096]{1,0:T(1,128)}, u32[]{:S(2)}) copy-start(f32[1,4096]{1,0:T(1,128)} %param.8) | copy-start | bytes 49156
  57.8 43.4 %copy-start = (bf16[1,4096,128]{1,2,0:T(8,128)(2,1)S(1)}, bf16[1,4096,128]{1,2,0:T(8,128)(2,1)}, u32[]{:S(2)}) copy-start(bf16[1,4096,128]{1,2,0:T(8,128)(2,1)} %copy.6) | copy-start | bytes 3145732
where the time goes:
time: 147 us
  blocking collectives  81.8 us (56%)
  local copies, waits for them, and re-layouts  28.3 us (19%)
  waiting for transfers between devices  14.3 us (10%)
  matrix products  11.3 us (8%)
  starting transfers between devices  7.92 us (5%)
  other arithmetic  2.32 us (2%)
    psum x2, blocking collectives, shards(): density = lax.psum(density, ('kx', 'ky'))  81.8 us
    gather x2, local copies, waits for them, and re-layouts, partner_of(): return (jnp.take(far_states, reorder[q_index, 0], axis=0), far_energy)  24.3 us
    ppermute x4, waiting for transfers between devices, passed_along(): return lax.ppermute(value, axis, pairs)  14.3 us
    dot_general x4, matrix products, respond(): jnp.einsum('gm,amn->agn', far_states, response_low, preferred_element_typ...  8.27 us
    ppermute x4, starting transfers between devices, passed_along(): return lax.ppermute(value, axis, pairs)  7.92 us
    unnamed x6, local copies, waits for them, and re-layouts  3.03 us
  transfers between devices with their start and end apart: 4, of which 1 were waited for; matrix products, arithmetic and copies ran while one was open for 13% of the time, Pallas kernels for 0%

commit v1 on v0

v1 whole, which is shorter than its diff:
```python
import functools
import math

import jax
import jax.numpy as jnp
import numpy as np
from jax import lax
from jax.experimental import pallas as pl
from jax.experimental.pallas import tpu as pltpu
from jax.sharding import PartitionSpec as P

GX = 64
ITERS = 2


SMEAR = 0.5
FERMI = 0.0
SCREEN = 4.0
PIECES = 8
ROWS = 32
MESH = pl.DeviceIdType.MESH


def hartley_table(length):
    positions = np.arange(length)
    angles = (positions[:, None] * positions[None, :] % length) * (2.0 * math.pi / length)
    return ((np.cos(angles) + np.sin(angles)) / math.sqrt(length)).astype(np.float32)


def screening(len_x, len_y):
    freq_x = np.arange(len_x)
    freq_x = np.minimum(freq_x, len_x - freq_x).astype(np.float32)
    freq_y = np.arange(len_y)
    freq_y = np.minimum(freq_y, len_y - freq_y).astype(np.float32)
    return 1.0 / (1.0 + (freq_x[:, None] ** 2 + freq_y[None, :] ** 2) / SCREEN)


def occupation(energy):
    return 1.0 / (1.0 + jnp.exp((energy - FERMI) / SMEAR))


def kernel(
    n_kx,
    n_ky,
    states,
    energy,
    reorder,
    external,
    table_x,
    table_y,
    screen,
    response_out,
    density_out,
    wide,
    stage,
    outgoing,
    far,
    far_energy,
    wanted,
    order,
    weighted,
    part,
    gathered,
    crossed,
    whole,
    order_send,
    order_recv,
    order_local,
    energy_send,
    energy_recv,
    rows_send,
    rows_recv,
    sum_send,
    sum_recv,
    cross_send,
    cross_recv,
    spread_send,
    spread_recv,
):
    grid, bands = states.shape
    nq = reorder.shape[0]
    len_y = grid // GX
    piece = grid // PIECES
    columns = GX // PIECES
    kx = lax.axis_index("kx")
    ky = lax.axis_index("ky")

    def remote(source, target, send, recv, where):
        return pltpu.make_async_remote_copy(
            src_ref=source, dst_ref=target, send_sem=send, recv_sem=recv, device_id=where, device_id_type=MESH
        )

    barrier = pltpu.get_barrier_semaphore()
    for step in range(1, n_kx):
        pl.semaphore_signal(barrier, inc=1, device_id={"kx": lax.rem(kx + step, n_kx)}, device_id_type=MESH)
    for step in range(1, n_ky):
        pl.semaphore_signal(barrier, inc=1, device_id={"ky": lax.rem(ky + step, n_ky)}, device_id_type=MESH)
    wide[...] = states[...].astype(jnp.float32)
    pl.semaphore_wait(barrier, n_kx + n_ky - 2)

    ahead = ({"kx": lax.rem(kx + 1, n_kx)}, {"ky": lax.rem(ky + 1, n_ky)})
    behind = ({"kx": lax.rem(kx + n_kx - 1, n_kx)}, {"ky": lax.rem(ky + n_ky - 1, n_ky)})

    orders = [
        remote(reorder.at[q], wanted.at[q], order_send.at[q], order_recv.at[q], ahead[q]) for q in range(nq)
    ]
    energies = [
        remote(energy, far_energy.at[q], energy_send.at[q], energy_recv.at[q], behind[q]) for q in range(nq)
    ]
    for q in range(nq):
        orders[q].start()
    for q in range(nq):
        energies[q].start()
    locals_ = [pltpu.make_async_copy(wanted.at[q], order.at[q], order_local.at[q]) for q in range(nq)]
    for q in range(nq):
        orders[q].wait_recv()
        locals_[q].start()
    for q in range(nq):
        locals_[q].wait()

    def rows_copy(q, c):
        rows = pl.ds(pl.multiple_of(c * piece, piece), piece)
        return remote(
            outgoing.at[q, rows], far.at[q, rows], rows_send.at[q, c], rows_recv.at[q, c], behind[q]
        )

    def send_piece(c, carry):
        for q in range(nq):

            def some_rows(b, inner):
                first = pl.multiple_of(c * piece + b * ROWS, ROWS)
                for half in range(0, ROWS, 16):
                    picked = [wide[pl.ds(order[q, 0, first + half + r], 1), :] for r in range(16)]
                    for r in range(16):
                        stage[half + r : half + r + 1, :] = picked[r]
                outgoing[q, pl.ds(first, ROWS), :] = stage[...].astype(jnp.bfloat16)
                return inner

            lax.fori_loop(0, piece // ROWS, some_rows, 0)
            rows_copy(q, c).start()
        return carry

    lax.fori_loop(0, PIECES, send_piece, 0)

    own = energy[0:1, :]
    weights = []
    for q in range(nq):
        energies[q].wait_recv()
        other = jnp.broadcast_to(far_energy[q, 0:1, :], (bands, bands)).T
        gap = other - own
        weights.append((occupation(own) - occupation(other)) * gap / (gap * gap + SMEAR * SMEAR))

    lanes = lax.broadcasted_iota(jnp.int32, (len_y, nq * GX), 1)

    def bands_of(q, potential, waits):
        def one(c, total):
            if waits:
                rows_copy(q, c).wait_recv()
            turned = pltpu.roll(potential, lax.rem(2 * nq * GX - q * GX - c * columns, nq * GX), 1)
            for x in range(columns):
                rows = pl.ds(pl.multiple_of(c * piece + x * len_y, len_y), len_y)
                scaled = turned[:, x : x + 1] * states[rows, :].astype(jnp.float32)
                weighted[x * len_y : (x + 1) * len_y, :] = scaled.astype(jnp.bfloat16)
            rows = pl.ds(pl.multiple_of(c * piece, piece), piece)
            return total + lax.dot_general(
                far[q, rows, :],
                weighted[...],
                (((0,), (0,)), ((), ())),
                preferred_element_type=jnp.float32,
            )

        return lax.fori_loop(0, PIECES, one, jnp.zeros((bands, bands), jnp.float32))

    def density_of(q, low, total):
        def one(c, total):
            rows = pl.ds(pl.multiple_of(c * piece, piece), piece)
            out = jnp.dot(far[q, rows, :], low, preferred_element_type=jnp.float32)
            out = out * states[rows, :].astype(jnp.float32)
            for x in range(columns):
                column = jnp.sum(out[x * len_y : (x + 1) * len_y, :], axis=1, keepdims=True)
                total = jnp.where(lanes == q * GX + c * columns + x, column, total)
            return total

        return lax.fori_loop(0, PIECES, one, total)

    scale = 1.0 / (math.sqrt(bands) * math.sqrt(n_kx * n_ky))

    def summed(rnd, total):
        part[rnd] = total.reshape(part.shape[1:])
        sends = []
        for d in range(1, n_ky):
            target = lax.rem(ky + d, n_ky)
            sends.append(
                remote(
                    part.at[rnd, target],
                    gathered.at[rnd, d],
                    sum_send.at[rnd, d],
                    sum_recv.at[rnd, d],
                    {"ky": target},
                )
            )
        for copy in sends:
            copy.start()
        mine = part[rnd, ky]
        for d, copy in enumerate(sends):
            copy.wait_recv()
            mine = mine + gathered[rnd, d + 1]
        crossed[rnd, kx] = mine
        crosses = []
        for d in range(1, n_kx):
            crosses.append(
                remote(
                    crossed.at[rnd, kx],
                    crossed.at[rnd, kx],
                    cross_send.at[rnd, d],
                    cross_recv.at[rnd, d],
                    {"kx": lax.rem(kx + d, n_kx)},
                )
            )
        for copy in crosses:
            copy.start()
        for copy in crosses:
            copy.wait_recv()
        mine = crossed[rnd, 0]
        for d in range(1, n_kx):
            mine = mine + crossed[rnd, d]
        whole[rnd, ky] = mine * scale
        spreads = []
        for d in range(1, n_ky):
            spreads.append(
                remote(
                    whole.at[rnd, ky],
                    whole.at[rnd, ky],
                    spread_send.at[rnd, d],
                    spread_recv.at[rnd, d],
                    {"ky": lax.rem(ky + d, n_ky)},
                )
            )
        for copy in spreads:
            copy.start()
        for copy in spreads:
            copy.wait_recv()
        return whole[rnd].reshape(total.shape), sends + crosses + spreads

    def exact(left, right):
        return jnp.dot(left, right, preferred_element_type=jnp.float32, precision=lax.Precision.HIGHEST)

    potential = external[...]
    pending = []
    for rnd in range(ITERS):
        total = jnp.zeros((len_y, nq * GX), jnp.float32)
        for q in reversed(range(nq)):
            mats = bands_of(q, potential, rnd == 0) * (1.0 / math.sqrt(grid))
            response = weights[q] * mats
            if rnd + 1 == ITERS:
                response_out[q] = response
            total = density_of(q, response.astype(jnp.bfloat16), total)
        density, sends = summed(rnd, total)
        pending = pending + sends
        if rnd + 1 < ITERS:
            spectrum = exact(exact(table_y[...], density), table_x[...]) * screen[...]
            potential = external[...] + exact(exact(table_y[...], spectrum), table_x[...])
    density_out[...] = density

    for q in range(nq):
        orders[q].wait_send()
        energies[q].wait_send()

    def drain(c, carry):
        for q in range(nq):
            rows_copy(q, c).wait_send()
        return carry

    lax.fori_loop(0, PIECES, drain, 0)
    for copy in pending:
        copy.wait_send()


def shards(n_kx, n_ky, states, energies, external, reorder):
    orbital = states[0]
    grid, bands = orbital.shape
    nq = reorder.shape[0]
    len_y = grid // GX
    energy = jnp.broadcast_to(energies.astype(jnp.float32), (8, bands))
    bare = jnp.tile(external.reshape(GX, len_y).T, (1, nq))
    table_x = jnp.asarray(np.kron(np.eye(nq, dtype=np.float32), hartley_table(GX)))
    table_y = jnp.asarray(hartley_table(len_y))
    screen = jnp.asarray(np.tile(screening(GX, len_y).T, (1, nq)).astype(np.float32))
    tall = len_y // n_ky
    wide = nq * GX
    vmem = pl.BlockSpec(memory_space=pltpu.VMEM)
    dma = pltpu.SemaphoreType.DMA
    response, density = pl.pallas_call(
        functools.partial(kernel, n_kx, n_ky),
        out_shape=(
            jax.ShapeDtypeStruct((nq, bands, bands), jnp.float32),
            jax.ShapeDtypeStruct((len_y, wide), jnp.float32),
        ),
        in_specs=[vmem, vmem, vmem, vmem, vmem, vmem, vmem],
        out_specs=(vmem, vmem),
        scratch_shapes=[
            pltpu.VMEM((grid, bands), jnp.float32),
            pltpu.VMEM((ROWS, bands), jnp.float32),
            pltpu.VMEM((nq, grid, bands), jnp.bfloat16),
            pltpu.VMEM((nq, grid, bands), jnp.bfloat16),
            pltpu.VMEM((nq, 8, bands), jnp.float32),
            pltpu.VMEM((nq, 1, grid), jnp.int32),
            pltpu.SMEM((nq, 1, grid), jnp.int32),
            pltpu.VMEM((grid // PIECES, bands), jnp.bfloat16),
            pltpu.VMEM((ITERS, n_ky, tall, wide), jnp.float32),
            pltpu.VMEM((ITERS, n_ky, tall, wide), jnp.float32),
            pltpu.VMEM((ITERS, n_kx, tall, wide), jnp.float32),
            pltpu.VMEM((ITERS, n_ky, tall, wide), jnp.float32),
            dma((nq,)),
            dma((nq,)),
            dma((nq,)),
            dma((nq,)),
            dma((nq,)),
            dma((nq, PIECES)),
            dma((nq, PIECES)),
            dma((ITERS, n_ky)),
            dma((ITERS, n_ky)),
            dma((ITERS, n_kx)),
            dma((ITERS, n_kx)),
            dma((ITERS, n_ky)),
            dma((ITERS, n_ky)),
        ],
        compiler_params=pltpu.CompilerParams(
            collective_id=0, has_side_effects=True, vmem_limit_bytes=40 * 2**20
        ),
        cost_estimate=pl.CostEstimate(flops=2**31, bytes_accessed=2**23, transcendentals=2**16),
    )(orbital, energy, reorder, bare, table_x, table_y, screen)
    density = density.reshape(len_y, nq, GX).transpose(1, 2, 0).reshape(nq, 1, grid)
    return (response[None, :, None], density)


def solution(mesh):
    return jax.shard_map(
        functools.partial(shards, mesh.shape["kx"], mesh.shape["ky"]),
        mesh=mesh,
        in_specs=(
            P(("kx", "ky"), None, None),
            P(("kx", "ky"), None),
            P(),
            P(None, ("kx", "ky"), None),
        ),
        out_specs=(P(("kx", "ky"), None, None, None, None), P()),
        check_vma=False,
    )
```

time: 147 us -> 78.7 us (0.54)
  blocking collectives: 81.8 us -> 0 us
  Pallas kernels: 0 us -> 71.4 us
  local copies, waits for them, and re-layouts: 28.3 us -> 4.98 us
  waiting for transfers between devices: 14.3 us -> 0 us
  matrix products: 11.3 us -> 0 us
  starting transfers between devices: 7.92 us -> 0 us
    psum x2 -> x0, blocking collectives: 81.8 us -> none  [shards(): density = lax.psum(density, ('kx', 'ky'))]
    pallas_call x0 -> x1, Pallas kernels: none -> 71.4 us  [shards(): pl.pallas_call(functools.partial(kernel, n_kx, n_ky), out_shape=(jax.Shap...]
    gather x2 -> x0, local copies, waits for them, and re-layouts: 24.3 us -> none  [partner_of(): return (jnp.take(far_states, reorder[q_index, 0], axis=0), far_energy)]
    ppermute x4 -> x0, waiting for transfers between devices: 14.3 us -> none  [passed_along(): return lax.ppermute(value, axis, pairs)]
    dot_general x10 -> x0, matrix products: 11.3 us -> none  [the longest x4 8.27 us: respond(): jnp.einsum('gm,amn->agn', far_states, response_low, preferred_element_typ...]
    ppermute x4 -> x0, starting transfers between devices: 7.92 us -> none  [passed_along(): return lax.ppermute(value, axis, pairs)]
    unnamed x6 -> x14, local copies, waits for them, and re-layouts: 3.03 us -> 3.79 us
  transfers between devices with their start and end apart: 4 -> 0, of which waited for: 1 -> 0; matrix products, arithmetic and copies ran while one was open for 13% -> 0% of each run, Pallas kernels for 0% -> 0%
where the time goes in v1:
time: 78.7 us; the launch traced here: 78.4 us
  Pallas kernels  71.4 us (91%)
  local copies, waits for them, and re-layouts  4.98 us (6%)
  other arithmetic  1.4 us (2%)
    pallas_call x1, Pallas kernels, shards(): pl.pallas_call(functools.partial(kernel, n_kx, n_ky), out_shape=(jax.Shap...  71.4 us
    unnamed x14, local copies, waits for them, and re-layouts  3.79 us

profile of v1, /device:TPU:0, one launch (start us, length us, event | category | flops | bytes accessed | tf_op | source)
XLA Modules:
  0.0 78.4 jit_solution(6175985641442118468)
XLA Ops:
  0.6 0.0 copy-start.5
  0.6 0.6 copy-done.5
  1.3 0.5 broadcast.6
  1.8 1.4 %reduce.3 = f32[4096]{0:T(1024)S(1)} reduce(f32[1,4096]{1,0:T(1,128)} %param.9, f32[]{:T(128)} %broadcast.6), dimensions={0}, to_apply=%param.9.reduce_sub_computation.3 | reduce | bytes 32772 | tf_op args[2]
  3.2 0.1 reshape.17
  3.3 0.1 copy.9
  3.4 0.0 copy-start.3
  3.4 0.0 copy-start.4
  3.4 0.0 copy-start.1
  3.4 0.0 copy-start.2
  3.4 0.1 tile.10.external
  3.5 0.6 copy-done.3
  4.1 0.0 copy-done.4
  4.1 0.0 copy-done.1
  4.2 0.1 copy-done.2
  4.3 0.0 copy-start
  4.3 1.2 %copy-done = bf16[1,4096,128]{2,1,0:T(8,128)(2,1)S(1)} copy-done((bf16[1,4096,128]{2,1,0:T(8,128)(2,1)S(1)}, bf16[1,4096,128]{2,1,0:T(8,128)(2,1)}, u32[]{:S(2)}) %copy-start) | copy-done | bytes 1048600
  5.5 71.4 %shard_map.86 = (f32[2,128,128]{2,1,0:T(8,128)S(1)}, f32[64,128]{1,0:T(8,128)S(1)}) custom-call(bf16[4096,128]{1,0:T(8,128)(2,1)S(1)} %bitcast.10, f32[8,128]{1,0:T(8,128)S(1)} %broadcast_in_dim.15.energy, s32[2,1,4096]{2,1,0:T(1,128)S(1)} %copy-done.1, f32[64,128]{1,0:T(8,128)S(1)} %tile.10.external, f32[128,128]{1,0:T(8,128)S(1)} %copy-done.2, ...), custom_call_target="tpu_custom_call" | custom-call | flops 2147483648 | bytes 8388608 | tf_op jit(solution)/shard_map/pallas_call | solution.py:293
  76.9 0.1 reshape.18
  77.0 0.1 copy.10
  77.1 0.7 reshape.19
  77.8 0.7 copy.13
  (3 shorter events, 0.0 us)
Async XLA Ops:
  0.6 0.7 copy-start.5
  3.4 0.8 copy-start.3
  3.4 0.8 copy-start.4
  3.4 0.8 copy-start.1
  3.4 0.9 %copy-start.2 = (f32[128,128]{1,0:T(8,128)S(1)}, f32[128,128]{1,0:T(8,128)}, u32[]{:S(2)}) copy-start(f32[128,128]{1,0:T(8,128)} %constant.6.clone.table_x) | copy-start | bytes 196612
  4.3 1.2 %copy-start = (bf16[1,4096,128]{2,1,0:T(8,128)(2,1)S(1)}, bf16[1,4096,128]{2,1,0:T(8,128)(2,1)}, u32[]{:S(2)}) copy-start(bf16[1,4096,128]{2,1,0:T(8,128)(2,1)} %param.7) | copy-start | bytes 3145732

commit v2 on v1

--- a/solution.py
+++ b/solution.py
@@ -18,6 +18,7 @@
 SCREEN = 4.0
 PIECES = 8
 ROWS = 32
+LANES = 128
 MESH = pl.DeviceIdType.MESH
 
 
@@ -43,14 +44,22 @@
     n_kx,
     n_ky,
     states,
-    energy,
+    energies_in,
     reorder,
     external,
-    table_x,
-    table_y,
+    along_y,
+    along_x,
+    back_x,
+    back_y,
     screen,
     response_out,
     density_out,
+    near,
+    turned,
+    energy,
+    potential,
+    bare,
+    dense,
     wide,
     stage,
     outgoing,
@@ -63,6 +72,7 @@
     gathered,
     crossed,
     whole,
+    states_sem,
     order_send,
     order_recv,
     order_local,
@@ -77,11 +87,12 @@
     spread_send,
     spread_recv,
 ):
-    grid, bands = states.shape
+    grid, bands = near.shape
     nq = reorder.shape[0]
-    len_y = grid // GX
     piece = grid // PIECES
-    columns = GX // PIECES
+    lines = grid // LANES
+    per = along_y.shape[0] // back_y.shape[0]
+    share = piece // LANES
     kx = lax.axis_index("kx")
     ky = lax.axis_index("ky")
 
@@ -90,12 +101,14 @@
             src_ref=source, dst_ref=target, send_sem=send, recv_sem=recv, device_id=where, device_id_type=MESH
         )
 
+    load = pltpu.make_async_copy(states, near, states_sem)
+    load.start()
+    energy[...] = jnp.broadcast_to(energies_in[...].astype(jnp.float32), energy.shape)
     barrier = pltpu.get_barrier_semaphore()
     for step in range(1, n_kx):
         pl.semaphore_signal(barrier, inc=1, device_id={"kx": lax.rem(kx + step, n_kx)}, device_id_type=MESH)
     for step in range(1, n_ky):
         pl.semaphore_signal(barrier, inc=1, device_id={"ky": lax.rem(ky + step, n_ky)}, device_id_type=MESH)
-    wide[...] = states[...].astype(jnp.float32)
     pl.semaphore_wait(barrier, n_kx + n_ky - 2)
 
     ahead = ({"kx": lax.rem(kx + 1, n_kx)}, {"ky": lax.rem(ky + 1, n_ky)})
@@ -111,6 +124,8 @@
         orders[q].start()
     for q in range(nq):
         energies[q].start()
+    load.wait()
+    wide[...] = near[...].astype(jnp.float32)
     locals_ = [pltpu.make_async_copy(wanted.at[q], order.at[q], order_local.at[q]) for q in range(nq)]
     for q in range(nq):
         orders[q].wait_recv()
@@ -142,46 +157,49 @@
 
     lax.fori_loop(0, PIECES, send_piece, 0)
 
-    own = energy[0:1, :]
+    def turn(c, carry):
+        rows = pl.ds(pl.multiple_of(c * piece, piece), piece)
+        turned[:, rows] = wide[rows, :].T.astype(jnp.bfloat16)
+        return carry
+
+    lax.fori_loop(0, PIECES, turn, 0)
+
+    own = jnp.broadcast_to(energy[0:1, :], (bands, bands)).T
     weights = []
     for q in range(nq):
         energies[q].wait_recv()
-        other = jnp.broadcast_to(far_energy[q, 0:1, :], (bands, bands)).T
+        other = far_energy[q, 0:1, :]
         gap = other - own
         weights.append((occupation(own) - occupation(other)) * gap / (gap * gap + SMEAR * SMEAR))
 
-    lanes = lax.broadcasted_iota(jnp.int32, (len_y, nq * GX), 1)
-
-    def bands_of(q, potential, waits):
+    def bands_of(q, waits):
         def one(c, total):
             if waits:
                 rows_copy(q, c).wait_recv()
-            turned = pltpu.roll(potential, lax.rem(2 * nq * GX - q * GX - c * columns, nq * GX), 1)
-            for x in range(columns):
-                rows = pl.ds(pl.multiple_of(c * piece + x * len_y, len_y), len_y)
-                scaled = turned[:, x : x + 1] * states[rows, :].astype(jnp.float32)
-                weighted[x * len_y : (x + 1) * len_y, :] = scaled.astype(jnp.bfloat16)
+            for t in range(share):
+                cut = pl.ds(pl.multiple_of(c * piece + t * LANES, LANES), LANES)
+                line = potential[pl.ds(q * lines + c * share + t, 1), :]
+                weighted[:, t * LANES : (t + 1) * LANES] = (line * turned[:, cut].astype(jnp.float32)).astype(
+                    jnp.bfloat16
+                )
             rows = pl.ds(pl.multiple_of(c * piece, piece), piece)
-            return total + lax.dot_general(
-                far[q, rows, :],
-                weighted[...],
-                (((0,), (0,)), ((), ())),
-                preferred_element_type=jnp.float32,
+            return total + jnp.dot(weighted[...], far[q, rows, :], preferred_element_type=jnp.float32)
+
+        return lax.fori_loop(0, PIECES, one, jnp.zeros((bands, bands), jnp.float32))
+
+    def density_of(q, low):
+        def one(c, carry):
+            rows = pl.ds(pl.multiple_of(c * piece, piece), piece)
+            out = lax.dot_general(
+                low, far[q, rows, :], (((1,), (1,)), ((), ())), preferred_element_type=jnp.float32
             )
-
-        return lax.fori_loop(0, PIECES, one, jnp.zeros((bands, bands), jnp.float32))
-
-    def density_of(q, low, total):
-        def one(c, total):
-            rows = pl.ds(pl.multiple_of(c * piece, piece), piece)
-            out = jnp.dot(far[q, rows, :], low, preferred_element_type=jnp.float32)
-            out = out * states[rows, :].astype(jnp.float32)
-            for x in range(columns):
-                column = jnp.sum(out[x * len_y : (x + 1) * len_y, :], axis=1, keepdims=True)
-                total = jnp.where(lanes == q * GX + c * columns + x, column, total)
-            return total
-
-        return lax.fori_loop(0, PIECES, one, total)
+            for t in range(share):
+                cut = pl.ds(pl.multiple_of(c * piece + t * LANES, LANES), LANES)
+                product = out[:, t * LANES : (t + 1) * LANES] * turned[:, cut].astype(jnp.float32)
+                dense[pl.ds(q * lines + c * share + t, 1), :] = jnp.sum(product, axis=0, keepdims=True)
+            return carry
+
+        lax.fori_loop(0, PIECES, one, 0)
 
     scale = 1.0 / (math.sqrt(bands) * math.sqrt(n_kx * n_ky))
 
@@ -245,21 +263,30 @@
     def exact(left, right):
         return jnp.dot(left, right, preferred_element_type=jnp.float32, precision=lax.Precision.HIGHEST)
 
-    potential = external[...]
+    for t in range(lines):
+        bare[t : t + 1, :] = external[:, t * LANES : (t + 1) * LANES]
+    for q in range(nq):
+        potential[q * lines : (q + 1) * lines, :] = bare[...]
     pending = []
     for rnd in range(ITERS):
-        total = jnp.zeros((len_y, nq * GX), jnp.float32)
         for q in reversed(range(nq)):
-            mats = bands_of(q, potential, rnd == 0) * (1.0 / math.sqrt(grid))
+            mats = bands_of(q, rnd == 0) * (1.0 / math.sqrt(grid))
             response = weights[q] * mats
             if rnd + 1 == ITERS:
-                response_out[q] = response
-            total = density_of(q, response.astype(jnp.bfloat16), total)
-        density, sends = summed(rnd, total)
+                response_out[q] = response.T
+            density_of(q, response.astype(jnp.bfloat16))
+        density, sends = summed(rnd, dense[...])
         pending = pending + sends
         if rnd + 1 < ITERS:
-            spectrum = exact(exact(table_y[...], density), table_x[...]) * screen[...]
-            potential = external[...] + exact(exact(table_y[...], spectrum), table_x[...])
+            mixed = exact(density, along_y[...])
+            spectrum = exact(along_x[...], jnp.concatenate(jnp.split(mixed, per, axis=1), axis=0))
+            filtered = exact(spectrum * screen[...], back_y[...])
+            spread = exact(back_x[...], filtered)
+            for q in range(nq):
+                line = jnp.concatenate(
+                    [spread[(q * per + b) * lines : (q * per + b + 1) * lines, :] for b in range(per)], axis=1
+                )
+                potential[q * lines : (q + 1) * lines, :] = bare[...] + line
     density_out[...] = density
 
     for q in range(nq):
@@ -281,24 +308,36 @@
     grid, bands = orbital.shape
     nq = reorder.shape[0]
     len_y = grid // GX
-    energy = jnp.broadcast_to(energies.astype(jnp.float32), (8, bands))
-    bare = jnp.tile(external.reshape(GX, len_y).T, (1, nq))
-    table_x = jnp.asarray(np.kron(np.eye(nq, dtype=np.float32), hartley_table(GX)))
-    table_y = jnp.asarray(hartley_table(len_y))
-    screen = jnp.asarray(np.tile(screening(GX, len_y).T, (1, nq)).astype(np.float32))
-    tall = len_y // n_ky
-    wide = nq * GX
+    lines = grid // LANES
+    per = LANES // len_y
+    hartley_x = hartley_table(GX)
+    hartley_y = hartley_table(len_y)
+    every_q = np.eye(nq, dtype=np.float32)
+    cut_x = hartley_x.reshape(GX, lines, per)
+    along_y = jnp.asarray(np.kron(np.eye(per, dtype=np.float32), hartley_y))
+    along_x = jnp.asarray(np.einsum("qs,ptb->qpbst", every_q, cut_x).reshape(nq * GX, per * nq * lines))
+    back_x = jnp.asarray(np.einsum("qs,ptb->qbtsp", every_q, cut_x).reshape(nq * per * lines, nq * GX))
+    back_y = jnp.asarray(hartley_y)
+    screen = jnp.asarray(np.tile(screening(GX, len_y), (nq, 1)).astype(np.float32))
+    tall = nq * lines // n_ky
     vmem = pl.BlockSpec(memory_space=pltpu.VMEM)
+    raw = pl.BlockSpec(memory_space=pl.ANY)
     dma = pltpu.SemaphoreType.DMA
     response, density = pl.pallas_call(
         functools.partial(kernel, n_kx, n_ky),
         out_shape=(
             jax.ShapeDtypeStruct((nq, bands, bands), jnp.float32),
-            jax.ShapeDtypeStruct((len_y, wide), jnp.float32),
+            jax.ShapeDtypeStruct((nq * lines, LANES), jnp.float32),
         ),
-        in_specs=[vmem, vmem, vmem, vmem, vmem, vmem, vmem],
+        in_specs=[raw, vmem, raw] + [vmem] * 6,
         out_specs=(vmem, vmem),
         scratch_shapes=[
+            pltpu.VMEM((grid, bands), jnp.bfloat16),
+            pltpu.VMEM((bands, grid), jnp.bfloat16),
+            pltpu.VMEM((8, bands), jnp.float32),
+            pltpu.VMEM((nq * lines, LANES), jnp.float32),
+            pltpu.VMEM((lines, LANES), jnp.float32),
+            pltpu.VMEM((nq * lines, LANES), jnp.float32),
             pltpu.VMEM((grid, bands), jnp.float32),
             pltpu.VMEM((ROWS, bands), jnp.float32),
             pltpu.VMEM((nq, grid, bands), jnp.bfloat16),
@@ -306,11 +345,12 @@
             pltpu.VMEM((nq, 8, bands), jnp.float32),
             pltpu.VMEM((nq, 1, grid), jnp.int32),
             pltpu.SMEM((nq, 1, grid), jnp.int32),
-            pltpu.VMEM((grid // PIECES, bands), jnp.bfloat16),
-            pltpu.VMEM((ITERS, n_ky, tall, wide), jnp.float32),
-            pltpu.VMEM((ITERS, n_ky, tall, wide), jnp.float32),
-            pltpu.VMEM((ITERS, n_kx, tall, wide), jnp.float32),
-            pltpu.VMEM((ITERS, n_ky, tall, wide), jnp.float32),
+            pltpu.VMEM((bands, grid // PIECES), jnp.bfloat16),
+            pltpu.VMEM((ITERS, n_ky, tall, LANES), jnp.float32),
+            pltpu.VMEM((ITERS, n_ky, tall, LANES), jnp.float32),
+            pltpu.VMEM((ITERS, n_kx, tall, LANES), jnp.float32),
+            pltpu.VMEM((ITERS, n_ky, tall, LANES), jnp.float32),
+            dma(()),
             dma((nq,)),
             dma((nq,)),
             dma((nq,)),
@@ -326,11 +366,11 @@
             dma((ITERS, n_ky)),
         ],
         compiler_params=pltpu.CompilerParams(
-            collective_id=0, has_side_effects=True, vmem_limit_bytes=40 * 2**20
+            collective_id=0, has_side_effects=True, vmem_limit_bytes=60 * 2**20
         ),
         cost_estimate=pl.CostEstimate(flops=2**31, bytes_accessed=2**23, transcendentals=2**16),
-    )(orbital, energy, reorder, bare, table_x, table_y, screen)
-    density = density.reshape(len_y, nq, GX).transpose(1, 2, 0).reshape(nq, 1, grid)
+    )(orbital, energies, reorder, external, along_y, along_x, back_x, back_y, screen)
+    density = density.reshape(nq, 1, grid)
     return (response[None, :, None], density)
 
 

time: 78.7 us -> 69.9 us (0.89)
  Pallas kernels: 71.4 us -> 66.9 us
  local copies, waits for them, and re-layouts: 4.98 us -> 2.19 us
  other arithmetic: 1.4 us -> 0 us
    pallas_call x1, Pallas kernels: 71.4 us -> 66.9 us  [shards(): pl.pallas_call(functools.partial(kernel, n_kx, n_ky), out_shape=(jax.Shap...]
    unnamed x14 -> x4, local copies, waits for them, and re-layouts: 3.79 us -> 2.19 us
    unnamed x1 -> x0, other arithmetic: 1.4 us -> none
    reshape x3 -> x0, local copies, waits for them, and re-layouts: 0.89 us -> none  [the longest x2 0.82 us: shards(): density.reshape(len_y, nq, GX).transpose(1, 2, 0).reshape(nq, 1, grid)]
where the time goes in v2:
time: 69.9 us; the launch traced here: 69.7 us
  Pallas kernels  66.9 us (96%)
  local copies, waits for them, and re-layouts  2.19 us (3%)
    pallas_call x1, Pallas kernels, shards(): pl.pallas_call(functools.partial(kernel, n_kx, n_ky), out_shape=(jax.Shap...  66.9 us
    unnamed x4, local copies, waits for them, and re-layouts  2.19 us

profile of v2, /device:TPU:0, one launch (start us, length us, event | category | flops | bytes accessed | tf_op | source)
XLA Modules:
  0.0 69.7 jit_solution(117695909894754014)
XLA Ops:
  0.6 66.9 %shard_map.104 = (f32[2,128,128]{2,1,0:T(8,128)}, f32[64,128]{1,0:T(8,128)}) custom-call(bf16[4096,128]{1,0:T(8,128)(2,1)} %bitcast.7, bf16[1,128]{1,0:T(2,128)(2,1)} %energies_in.1, s32[2,1,4096]{2,1,0:T(1,128)} %reorder.1, f32[1,4096]{1,0:T(1,128)} %external.1, f32[128,128]{1,0:T(8,128)} %constant.10.clone.along_y, f32[128,128]{1,0:T(8,128)} %constant.11.clone.along_x, ...), custom_call_target="tpu_custom_call" | custom-call | flops 2147483648 | bytes 8388608 | tf_op jit(solution)/shard_map/pallas_call | solution.py:326
  67.5 0.0 copy-start
  67.6 1.6 %copy.15 = f32[1,2,1,128,128]{4,3,2,1,0:T(8,128)} copy(f32[1,2,1,128,128]{4,3,2,1,0:T(8,128)} %bitcast.5) | data formatting | bytes 262144
  69.1 0.0 copy-done
  69.1 0.6 copy.16
Async XLA Ops:
  67.5 1.6 %copy-start = (f32[64,128]{1,0:T(8,128)S(1)}, f32[64,128]{1,0:T(8,128)}, u32[]{:S(2)}) copy-start(f32[64,128]{1,0:T(8,128)} %get-tuple-element.5) | copy-start | bytes 98308

commit v3 on v2

--- a/solution.py
+++ b/solution.py
@@ -185,7 +185,7 @@
             rows = pl.ds(pl.multiple_of(c * piece, piece), piece)
             return total + jnp.dot(weighted[...], far[q, rows, :], preferred_element_type=jnp.float32)
 
-        return lax.fori_loop(0, PIECES, one, jnp.zeros((bands, bands), jnp.float32))
+        return lax.fori_loop(0, PIECES, one, jnp.zeros((bands, bands), jnp.float32), unroll=True)
 
     def density_of(q, low):
         def one(c, carry):
@@ -199,7 +199,7 @@
                 dense[pl.ds(q * lines + c * share + t, 1), :] = jnp.sum(product, axis=0, keepdims=True)
             return carry
 
-        lax.fori_loop(0, PIECES, one, 0)
+        lax.fori_loop(0, PIECES, one, 0, unroll=True)
 
     scale = 1.0 / (math.sqrt(bands) * math.sqrt(n_kx * n_ky))
 

time: 69.9 us -> 64.3 us (0.920)
  Pallas kernels: 66.9 us -> 61.3 us
    pallas_call x1, Pallas kernels: 66.9 us -> 61.3 us  [shards(): pl.pallas_call(functools.partial(kernel, n_kx, n_ky), out_shape=(jax.Shap...]
where the time goes in v3:
time: 64.3 us; the launch traced here: 64.1 us
  Pallas kernels  61.3 us (95%)
  local copies, waits for them, and re-layouts  2.19 us (3%)
  between operations  0.65 us (1%)
    pallas_call x1, Pallas kernels, shards(): pl.pallas_call(functools.partial(kernel, n_kx, n_ky), out_shape=(jax.Shap...  61.3 us
    unnamed x4, local copies, waits for them, and re-layouts  2.19 us

profile of v3, /device:TPU:0, one launch (start us, length us, event | category | flops | bytes accessed | tf_op | source)
XLA Modules:
  0.0 64.1 jit_solution(11850839257777682748)
XLA Ops:
  0.6 61.3 %shard_map.104 = (f32[2,128,128]{2,1,0:T(8,128)}, f32[64,128]{1,0:T(8,128)}) custom-call(bf16[4096,128]{1,0:T(8,128)(2,1)} %bitcast.7, bf16[1,128]{1,0:T(2,128)(2,1)} %energies_in.1, s32[2,1,4096]{2,1,0:T(1,128)} %reorder.1, f32[1,4096]{1,0:T(1,128)} %external.1, f32[128,128]{1,0:T(8,128)} %constant.10.clone.along_y, f32[128,128]{1,0:T(8,128)} %constant.11.clone.along_x, ...), custom_call_target="tpu_custom_call" | custom-call | flops 2147483648 | bytes 8388608 | tf_op jit(solution)/shard_map/pallas_call | solution.py:326
  61.9 0.0 copy-start
  61.9 1.6 %copy.15 = f32[1,2,1,128,128]{4,3,2,1,0:T(8,128)} copy(f32[1,2,1,128,128]{4,3,2,1,0:T(8,128)} %bitcast.5) | data formatting | bytes 262144
  63.5 0.0 copy-done
  63.5 0.6 copy.16
Async XLA Ops:
  61.9 1.6 %copy-start = (f32[64,128]{1,0:T(8,128)S(1)}, f32[64,128]{1,0:T(8,128)}, u32[]{:S(2)}) copy-start(f32[64,128]{1,0:T(8,128)} %get-tuple-element.5) | copy-start | bytes 98308
